TPU v7x, 512 devices: a whole 4x4x16 slice. The times are simulated.
512 devices in a mesh: seq: 64 (over z, y_lo, core), head: 8 (over y_hi, x).
Axes of the slice: x: 4, y: 4 (y_hi: 2, y_lo: 2; y = y_hi * 2 + y_lo), z: 16, core: 2. Of those that a mesh axis runs over, the one named last changes fastest.
Arguments:
- query_states: bfloat16 [8192, 3072], P(('seq', 'head')), may hold values from -48 to 48
- key_states: bfloat16 [8192, 3072], P(('seq', 'head')), may hold values from -9 to 9
- value_states: bfloat16 [8192, 3072], P(('seq', 'head')), may hold values from -6 to 6
- base_patch: bfloat16 [8192, 64], P(('seq', 'head')), may hold values from -4 to 4
- head_proj: bfloat16 [3072, 64], P('head'), may hold values from -0.4375 to 0.4375
- latent_std: float32 [16], replicated, may hold values from 0.5 to 2
- latent_mean: float32 [16], replicated, may hold values from -1 to 1
- w_in: bfloat16 [3, 3, 3, 16, 384], replicated, may hold values from -0.3125 to 0.3125
- b_in: float32 [384], replicated, may hold values from -0.5 to 0.5
- gain_mid: float32 [384], replicated, may hold values from 0.25 to 1.75
- w_up: bfloat16 [3, 3, 384, 192], replicated, may hold values from -0.109375 to 0.109375
- b_up: float32 [192], replicated, may hold values from -0.5 to 0.5
Outputs:
- video_features: bfloat16 [16, 256, 32, 192], P('head', 'seq')
All inputs are finite; a program needn't handle non-finite values.
Results may differ from a plain program's by a relative error of at most 0.017.
Values may be sent and summed in bfloat16 or wider, within the bound.
A program may use at most 64 MiB of HBM per device.

v0:
```python
import math

import jax
import jax.numpy as jnp
from jax import lax
from jax.sharding import PartitionSpec as P

HD = 128
LATENT_CH = 16
WP = 8


def passed_along(block, axis, distance):
    devices = range(lax.axis_size(axis))
    route = [(i - distance, i) for i in devices if i - distance in devices]
    return lax.ppermute(block, axis, route)


def with_halo(value, sides, width):
    for axis, dim in sides:
        size, length = (lax.axis_size(axis), value.shape[dim])
        up = [(i, (i + 1) % size) for i in range(size - 1)]
        down = [(j, i) for i, j in up]
        last = lax.slice_in_dim(value, length - width, length, axis=dim)
        leading = lax.slice_in_dim(value, 0, width, axis=dim)
        before = lax.ppermute(last, axis, up)
        after = lax.ppermute(leading, axis, down)
        value = jnp.concatenate([before, value, after], axis=dim)
    return value


def conv_volume(padded, kernel):
    return lax.conv_general_dilated(
        padded[None],
        kernel,
        (1, 1, 1),
        "VALID",
        dimension_numbers=("NDHWC", "DHWIO", "NDHWC"),
        preferred_element_type=jnp.float32,
    )[0]


def conv_plane(padded, kernel):
    return lax.conv_general_dilated(
        padded,
        kernel,
        (1, 1),
        "VALID",
        dimension_numbers=("NHWC", "HWIO", "NHWC"),
        preferred_element_type=jnp.float32,
    )


def rms_silu(conv_out, gain_mid):
    mean_sq = jnp.mean(conv_out * conv_out, axis=-1, keepdims=True)
    normed = conv_out * lax.rsqrt(mean_sq + 1e-06) * gain_mid
    return jax.nn.silu(normed).astype(jnp.bfloat16)


def enlarge(field):
    return jnp.repeat(jnp.repeat(field, 2, axis=1), 2, axis=2)


def on_device(
    query_states,
    key_states,
    value_states,
    base_patch,
    head_proj,
    latent_std,
    latent_mean,
    w_in,
    b_in,
    gain_mid,
    w_up,
    b_up,
):
    q_rows, k_rows, v_rows = (
        lax.all_to_all(query_states, "head", split_axis=1, concat_axis=0, tiled=True),
        lax.all_to_all(key_states, "head", split_axis=1, concat_axis=0, tiled=True),
        lax.all_to_all(value_states, "head", split_axis=1, concat_axis=0, tiled=True),
    )
    row_count = q_rows.shape[0]
    local_heads = q_rows.shape[1] // HD
    scaling = 1.0 / math.sqrt(HD)
    queries3 = q_rows.reshape(row_count, local_heads, HD)
    initial = (
        jnp.full((local_heads, row_count), -1e30, jnp.float32),
        jnp.zeros((local_heads, row_count), jnp.float32),
        jnp.zeros((local_heads, row_count, HD), jnp.float32),
    )
    key_piece = lax.all_gather(k_rows, "seq", axis=0, tiled=True)
    value_piece = lax.all_gather(v_rows, "seq", axis=0, tiled=True)
    length = key_piece.shape[0]
    block_len = math.gcd(length, 1024)
    key_blocks = key_piece.reshape(length // block_len, block_len, local_heads, HD)
    value_blocks = value_piece.reshape(length // block_len, block_len, local_heads, HD)

    def one_step(running, blocked):
        running_max, totals, summed = running
        key_block, value_block = blocked
        scores = (
            jnp.einsum("qhd,khd->hqk", queries3, key_block, preferred_element_type=jnp.float32)
            * scaling
        )
        new_max = jnp.maximum(running_max, jnp.max(scores, axis=2))
        fading = jnp.exp(running_max - new_max)
        weights = jnp.exp(scores - new_max[:, :, None])
        totals = totals * fading + jnp.sum(weights, axis=2)
        summed = summed * fading[:, :, None] + jnp.einsum(
            "hqk,khd->hqd",
            weights.astype(jnp.bfloat16),
            value_block,
            preferred_element_type=jnp.float32,
        )
        return ((new_max, totals, summed), None)

    result, unused = lax.scan(one_step, initial, (key_blocks, value_blocks))
    attended = (result[2] / result[1][:, :, None]).astype(jnp.bfloat16)
    attended = attended.transpose(1, 0, 2).reshape(row_count, local_heads * HD)
    regrouped = lax.all_to_all(attended, "head", split_axis=0, concat_axis=1, tiled=True)
    full_proj = lax.all_gather(head_proj, "head", axis=0, tiled=True)
    patch = base_patch.astype(jnp.float32) + jnp.dot(
        regrouped, full_proj, preferred_element_type=jnp.float32
    )
    tile_frames = base_patch.shape[0] // WP
    latent_tile = (
        patch.reshape(tile_frames, WP, 2, 2, LATENT_CH)
        .transpose(0, 2, 1, 3, 4)
        .reshape(tile_frames, 2, 2 * WP, LATENT_CH)
    )
    latent_tile = (latent_tile * latent_std + latent_mean).astype(jnp.bfloat16)
    earlier = passed_along(latent_tile, "head", 1)
    stacked = jnp.concatenate([earlier, latent_tile], axis=0)
    rimmed = with_halo(stacked, (("seq", 1),), 1)
    conv_out = conv_volume(jnp.pad(rimmed, ((0, 0), (0, 0), (1, 1), (0, 0))), w_in) + b_in
    activated = rms_silu(conv_out, gain_mid)
    enlarged = with_halo(enlarge(activated), (("seq", 1),), 1)
    planes = conv_plane(jnp.pad(enlarged, ((0, 0), (0, 0), (1, 1), (0, 0))), w_up) + b_up
    return planes.astype(jnp.bfloat16)


def solution(mesh):
    in_specs = (
        P(("seq", "head"), None),
        P(("seq", "head"), None),
        P(("seq", "head"), None),
        P(("seq", "head"), None),
        P("head", None),
        P(),
        P(),
        P(),
        P(),
        P(),
        P(),
        P(),
    )
    out_specs = P("head", "seq", None, None)
    return jax.shard_map(
        on_device, mesh=mesh, in_specs=in_specs, out_specs=out_specs, check_vma=False
    )
```

profile of v0, /device:TPU:1, one launch (start us, length us, event | category | flops | bytes accessed | tf_op | source)
XLA Modules:
  0.0 404.4 jit_solution(8611973332948445407)
XLA Ops:
  6.5 1.0 copy.120
  7.6 14.2 %all_to_all.73 = bf16[16,8,384]{2,0,1:T(8,128)(2,1)} all-to-all(bf16[16,8,384]{2,0,1:T(8,128)(2,1)S(1)} %bitcast.98), channel_id=1, replica_groups=mesh['seq'=64,'head'=8] {'head'}, dimensions={1} | all-to-all | bytes 196608 | tf_op jit(solution)/shard_map/all_to_all | solution.py:80
  21.8 0.9 copy.118
  22.7 9.9 %all_to_all.74 = bf16[16,8,384]{2,0,1:T(8,128)(2,1)} all-to-all(bf16[16,8,384]{2,0,1:T(8,128)(2,1)S(1)} %bitcast.99), channel_id=1, replica_groups=mesh['seq'=64,'head'=8] {'head'}, dimensions={1} | all-to-all | bytes 196608 | tf_op jit(solution)/shard_map/all_to_all | solution.py:81
  32.6 1.5 copy.119
  34.1 3.4 all-to-all-start.1
  37.5 6.7 %all-to-all-done.1 = bf16[16,8,384]{2,0,1:T(8,128)(2,1)S(1)} async-done(((bf16[16,8,384]{2,0,1:T(8,128)(2,1)}), bf16[16,8,384]{2,0,1:T(8,128)(2,1)S(1)}, u32[]{:S(2)}, u32[]{:S(2)}) %all-to-all-start.1) | async-done | bytes 98336 | tf_op jit(solution)/shard_map/all_to_all | solution.py:79
  44.3 106.7 %all-gather.3.cloned.1.call-done = bf16[8192,384]{1,0:T(8,128)(2,1)} async-done(((bf16[128,384]{1,0:T(8,128)(2,1)}), bf16[8192,384]{1,0:T(8,128)(2,1)}) %all-gather.3.cloned.1.call-update) | async-done | bytes 6291472 | tf_op jit(solution)/shard_map/all_gather | solution.py:92
  151.0 16.7 %reshape.83 = bf16[8,1024,3,128]{3,2,1,0:T(4,128)(2,1)} reshape(bf16[8192,384]{1,0:T(8,128)(2,1)} %all-gather.3.cloned.1.call-done) | data formatting | bytes 12582912 | tf_op jit(solution)/shard_map/reshape | solution.py:96
  167.7 7.8 %copy.78 = bf16[8,1024,3,128]{3,1,2,0:T(8,128)(2,1)} copy(bf16[8,1024,3,128]{3,2,1,0:T(4,128)(2,1)} %reshape.83) | data formatting | bytes 12582912
  175.5 101.1 %all-gather.5.cloned.1.call-done = bf16[8192,384]{1,0:T(8,128)(2,1)} async-done(((bf16[128,384]{1,0:T(8,128)(2,1)}), bf16[8192,384]{1,0:T(8,128)(2,1)}) %all-gather.5.cloned.1.call-update) | async-done | bytes 6291472 | tf_op jit(solution)/shard_map/all_gather | solution.py:93
  276.6 16.7 %reshape.84 = bf16[8,1024,3,128]{3,2,1,0:T(4,128)(2,1)} reshape(bf16[8192,384]{1,0:T(8,128)(2,1)} %all-gather.5.cloned.1.call-done) | data formatting | bytes 12582912 | tf_op jit(solution)/shard_map/reshape | solution.py:97
  293.3 7.6 %copy.80 = bf16[8,1024,3,128]{3,1,2,0:T(8,128)(2,1)} copy(bf16[8,1024,3,128]{3,2,1,0:T(4,128)(2,1)} %reshape.84) | data formatting | bytes 12582912
  300.8 27.6 %while.15 = (s32[]{:T(128)}, f32[3,128]{1,0:T(4,128)S(1)}, f32[3,128]{1,0:T(4,128)S(1)}, f32[3,128,128]{2,1,0:T(8,128)S(1)}, bf16[8,1024,3,128]{3,1,2,0:T(8,128)...) while((s32[]{:T(128)}, f32[3,128]{1,0:T(4,128)S(1)}, ...), condition=%wide.region_3.4_spmd.clone, body=%wide.region_0.3_spmd.clone.sunk | while | flops 203835264 | bytes 6808681 | solution.py:118
  300.8 1.5 bitcast_reduce_fusion.2
  302.6 1.6 convolution_add_fusion.3
  304.3 1.5 bitcast_reduce_fusion.2
  305.8 0.2 fusion.50
  306.1 1.6 convolution_add_fusion.3
  307.7 1.5 bitcast_reduce_fusion.2
  309.5 1.6 convolution_add_fusion.3
  311.2 1.5 bitcast_reduce_fusion.2
  313.0 1.6 convolution_add_fusion.3
  314.6 1.5 bitcast_reduce_fusion.2
  316.4 1.6 convolution_add_fusion.3
  318.1 1.5 bitcast_reduce_fusion.2
  319.9 1.6 convolution_add_fusion.3
  321.5 1.5 bitcast_reduce_fusion.2
  323.3 1.6 convolution_add_fusion.3
  325.0 1.5 bitcast_reduce_fusion.2
  326.8 1.6 convolution_add_fusion.3
  328.7 0.7 all_to_all.65
  329.5 6.1 %all-to-all-start.3 = ((bf16[8,16,384]{2,1,0:T(8,128)(2,1)}), bf16[8,16,384]{2,1,0:T(8,128)(2,1)S(1)}, u32[]{:S(2)}, u32[]{:S(2)}) async-start(bf16[8,16,384]{2,1,0:T(8,128)(2,1)} %all_to_all.65), calls=%async_computation.3 | async-start | bytes 196608 | tf_op jit(solution)/shard_map/all_to_all | solution.py:121
  335.6 29.9 %all_gather.11 = bf16[3072,64]{0,1:T(8,128)(2,1)S(1)} all-gather(bf16[384,64]{0,1:T(8,128)(2,1)S(1)} %copy-done.1), channel_id=1, replica_groups=mesh['seq'=64,'head'=8] {'head'}, dimensions={0}, use_global_device_ids=true | all-gather | bytes 442368 | tf_op jit(solution)/shard_map/all_gather | solution.py:122
  365.9 2.3 collective-permute-start
  368.2 0.9 collective-permute-done
  369.1 9.5 %collective-permute-start.1 = (bf16[4,1,16,16]{3,2,1,0:T(8,128)(2,1)S(1)}, bf16[4,1,16,16]{3,2,1,0:T(8,128)(2,1)S(1)}, u32[]{:S(2)}, u32[]{:S(2)}) collective-permute-start(bf16[4,1,16,16]{3,2,1,0:T(8,128)(2,1)S(1)} %get-tuple-element.117), channel_id=1, source_target_pairs={{0,8},{8,16},{16,24},{24,32},{32,40},{40,48},{48,56},{56,64},{64,7... | collective-permute-start | bytes 6152 | tf_op jit(solution)/shard_map/ppermute | solution.py:26
  378.6 1.9 collective-permute-start.2
  380.6 3.1 collective-permute-done.2
  383.9 0.6 convolution_select_fusion.1
  385.2 2.4 collective-permute-start.3
  387.6 1.9 collective-permute-start.4
  389.6 5.1 %collective-permute-done.4 = bf16[2,1,32,384]{3,0,2,1:T(2,128)(2,1)S(1)} collective-permute-done((bf16[2,1,32,384]{3,0,2,1:T(2,128)(2,1)S(1)}, bf16[2,1,32,384]{3,0,2,1:T(2,128)(2,1)S(1)}, u32[]{:S(2)}, u32[]{:S(2)}) %collective-permute-start.4) | collective-permute-done | bytes 49184 | tf_op jit(solution)/shard_map/ppermute | solution.py:27
  394.7 0.4 maximum_bitcast_fusion
  395.1 0.3 pad.9
  395.5 0.4 fusion.14
  396.0 0.8 fusion.13
  396.9 0.7 copy.92
  (90 shorter events, 3.6 us)
Async XLA Ops:
  6.5 389.4 %copy-start = (bf16[3,3,384,192]{2,3,1,0:T(8,128)(2,1)S(1)}, bf16[3,3,384,192]{2,3,1,0:T(8,128)(2,1)}, u32[]{:S(2)}) copy-start(bf16[3,3,384,192]{2,3,1,0:T(8,128)(2,1)} %param.24) | copy-start | bytes 3981316
  6.5 144.5 %all-gather.3.cloned.1.call-start = ((), (), s32[]{:S(2)}) async-start(), calls=%async_computation.4 | async-start | bytes 6389760 | tf_op jit(solution)/shard_map/all_gather | solution.py:92
  21.7 254.9 %all-gather.5.cloned.1.call-start = ((), (), s32[]{:S(2)}) async-start(), calls=%async_computation.5 | async-start | bytes 6389760 | tf_op jit(solution)/shard_map/all_gather | solution.py:93
  34.1 10.1 %all-to-all-start.1 = ((bf16[16,8,384]{2,0,1:T(8,128)(2,1)}), bf16[16,8,384]{2,0,1:T(8,128)(2,1)S(1)}, u32[]{:S(2)}, u32[]{:S(2)}) async-start(bf16[16,8,384]{2,0,1:T(8,128)(2,1)} %bitcast.74), calls=%async_computation.1 | async-start | bytes 196608 | tf_op jit(solution)/shard_map/all_to_all | solution.py:79
  300.8 34.8 %copy-start.1 = (bf16[384,64]{0,1:T(8,128)(2,1)S(1)}, bf16[384,64]{0,1:T(8,128)(2,1)}, u32[]{:S(2)}) copy-start(bf16[384,64]{0,1:T(8,128)(2,1)} %param.18) | copy-start | bytes 147460
  328.4 37.1 %copy-start.3 = (bf16[16,64]{1,0:T(8,128)(2,1)S(1)}, bf16[16,64]{1,0:T(8,128)(2,1)}, u32[]{:S(2)}) copy-start(bf16[16,64]{1,0:T(8,128)(2,1)} %param.17) | copy-start | bytes 6148
  328.5 37.4 %copy-start.5 = (f32[16]{0:T(128)S(1)}, f32[16]{0:T(128)}, u32[]{:S(2)}) copy-start(f32[16]{0:T(128)} %param.20) | copy-start | bytes 196
  328.5 37.4 %copy-start.6 = (f32[16]{0:T(128)S(1)}, f32[16]{0:T(128)}, u32[]{:S(2)}) copy-start(f32[16]{0:T(128)} %param.19) | copy-start | bytes 196
  328.5 55.4 %copy-start.7 = (bf16[3,3,3,16,384]{4,3,2,1,0:T(8,128)(2,1)S(1)}, bf16[3,3,3,16,384]{4,3,2,1,0:T(8,128)(2,1)}, u32[]{:S(2)}) copy-start(bf16[3,3,3,16,384]{4,3,2,1,0:T(8,128)(2,1)} %param.21) | copy-start | bytes 995332
  328.5 55.4 %copy-start.10 = (pred[8,3]{0,1:T(4,128)(4,1)S(1)}, pred[8,3]{0,1:T(4,128)(4,1)}, u32[]{:S(2)}) copy-start(pred[8,3]{0,1:T(4,128)(4,1)} %constant.47) | copy-start | bytes 76
  329.5 36.0 %all-to-all-start.3 = ((bf16[8,16,384]{2,1,0:T(8,128)(2,1)}), bf16[8,16,384]{2,1,0:T(8,128)(2,1)S(1)}, u32[]{:S(2)}, u32[]{:S(2)}) async-start(bf16[8,16,384]{2,1,0:T(8,128)(2,1)} %all_to_all.65), calls=%async_computation.3 | async-start | bytes 196608 | tf_op jit(solution)/shard_map/all_to_all | solution.py:121
  365.9 3.2 collective-permute-start
  369.1 11.5 %collective-permute-start.1 = (bf16[4,1,16,16]{3,2,1,0:T(8,128)(2,1)S(1)}, bf16[4,1,16,16]{3,2,1,0:T(8,128)(2,1)S(1)}, u32[]{:S(2)}, u32[]{:S(2)}) collective-permute-start(bf16[4,1,16,16]{3,2,1,0:T(8,128)(2,1)S(1)} %get-tuple-element.117), channel_id=1, source_target_pairs={{0,8},{8,16},{16,24},{24,32},{32,40},{40,48},{48,56},{56,64},{64,7... | collective-permute-start | bytes 6152 | tf_op jit(solution)/shard_map/ppermute | solution.py:26
  378.6 6.0 %copy-start.2 = (f32[384]{0:T(512)S(1)}, f32[384]{0:T(512)}, u32[]{:S(2)}) copy-start(f32[384]{0:T(512)} %param.22) | copy-start | bytes 4612
  378.6 5.1 %collective-permute-start.2 = (bf16[4,1,16,16]{3,2,1,0:T(8,128)(2,1)S(1)}, bf16[4,1,16,16]{3,2,1,0:T(8,128)(2,1)S(1)}, u32[]{:S(2)}, u32[]{:S(2)}) collective-permute-start(bf16[4,1,16,16]{3,2,1,0:T(8,128)(2,1)S(1)} %get-tuple-element.118), channel_id=1, source_target_pairs={{8,0},{16,8},{24,16},{32,24},{40,32},{48,40},{56,48},{64,56},{72,6... | collective-permute-start | bytes 6152 | tf_op jit(solution)/shard_map/ppermute | solution.py:27
  383.7 1.0 copy-start.4
  385.0 11.0 %copy-start.8 = (f32[192]{0:T(256)S(1)}, f32[192]{0:T(256)}, u32[]{:S(2)}) copy-start(f32[192]{0:T(256)} %param.25) | copy-start | bytes 2308
  385.0 11.0 %copy-start.9 = (pred[16,5]{0,1:T(8,128)(4,1)S(1)}, pred[16,5]{0,1:T(8,128)(4,1)}, u32[]{:S(2)}) copy-start(pred[16,5]{0,1:T(8,128)(4,1)} %constant.46) | copy-start | bytes 244
  385.2 4.3 %collective-permute-start.3 = (bf16[2,1,32,384]{3,0,2,1:T(2,128)(2,1)S(1)}, bf16[2,1,32,384]{3,0,2,1:T(2,128)(2,1)S(1)}, u32[]{:S(2)}, u32[]{:S(2)}) collective-permute-start(bf16[2,1,32,384]{3,0,2,1:T(2,128)(2,1)S(1)} %get-tuple-element.115), channel_id=1, source_target_pairs={{0,8},{8,16},{16,24},{24,32},{32,40},{40,48},{48,56},{56,64},{64,7... | collective-permute-start | bytes 147464 | tf_op jit(solution)/shard_map/ppermute | solution.py:26
  387.6 7.1 %collective-permute-start.4 = (bf16[2,1,32,384]{3,0,2,1:T(2,128)(2,1)S(1)}, bf16[2,1,32,384]{3,0,2,1:T(2,128)(2,1)S(1)}, u32[]{:S(2)}, u32[]{:S(2)}) collective-permute-start(bf16[2,1,32,384]{3,0,2,1:T(2,128)(2,1)S(1)} %get-tuple-element.116), channel_id=1, source_target_pairs={{8,0},{16,8},{24,16},{32,24},{40,32},{48,40},{56,48},{64,56},{72,6... | collective-permute-start | bytes 147464 | tf_op jit(solution)/shard_map/ppermute | solution.py:27
Sparse Core Ops, SparseCore 0:
  21.9 129.1 all-gather.2
  153.2 123.3 all-gather.4
where the time goes:
time: 411 us; the launch traced here: 404 us
  waiting for transfers between devices  224 us (55%)
  local copies, waits for them, and re-layouts  54.8 us (13%)
  blocking collectives  53.9 us (13%)
  starting transfers between devices  27.6 us (7%)
  matrix products  26.8 us (7%)
  between operations  13.9 us (3%)
    all_gather x1, waiting for transfers between devices, on_device(): key_piece = lax.all_gather(k_rows, 'seq', axis=0, tiled=True)  107 us
    all_gather x1, waiting for transfers between devices, on_device(): value_piece = lax.all_gather(v_rows, 'seq', axis=0, tiled=True)  101 us
    all_gather x1, blocking collectives, on_device(): full_proj = lax.all_gather(head_proj, 'head', axis=0, tiled=True)  29.9 us
    reshape x1, local copies, waits for them, and re-layouts, on_device(): key_piece.reshape(length // block_len, block_len, local_heads, HD)  16.7 us
    reshape x1, local copies, waits for them, and re-layouts, on_device(): value_piece.reshape(length // block_len, block_len, local_heads, HD)  16.7 us
    unnamed x26, local copies, waits for them, and re-layouts  15.5 us
    all_to_all x1, blocking collectives, on_device(): lax.all_to_all(key_states, 'head', split_axis=1, concat_axis=0, tiled=True)  14.2 us
    dot_general x8, matrix products, one_step(): jnp.einsum('hqk,khd->hqd', weights.astype(jnp.bfloat16), value_block, pre...  13.1 us
  transfers between devices with their start and end apart: 9, of which 6 were waited for; matrix products, arithmetic and copies ran while one was open for 7% of the time, Pallas kernels for 0%

commit v1 on v0

v1 whole, which is shorter than its diff:
```python
import math

import jax
import jax.numpy as jnp
from jax import lax
from jax.experimental import pallas as pl
from jax.experimental.pallas import tpu as pltpu
from jax.sharding import PartitionSpec as P

MESH = pl.DeviceIdType.MESH
F32, BF16 = jnp.float32, jnp.bfloat16

SEQ, GROUPS = 64, 8
ROWS = 4
PLACES = ROWS * GROUPS
OWN = 16
ROW = OWN * GROUPS
PLANE = ROW * ROWS
HD, LOCAL = 128, 3
WIDE = HD * LOCAL
PATCH = 64
NUM = PATCH * LOCAL
MSG = 256
CH, OUTCH = 384, 192
EDGE = 8
LINE = 48
TO_LOG2 = math.log2(math.e) / math.sqrt(HD)


def dot(a, b, dims):
    return lax.dot_general(a, b, (dims, ((), ())), preferred_element_type=F32)


def kernel(
    q_in, k_in, v_in, base_ref, proj_ref, std_ref, mean_ref, w_in_any, b_in_ref, gain_ref, w_up_any, b_up_ref,
    out_ref,
    kv, queries, top, total, summed, turned, sending, parts, lat_own, lat_near, w_in, w_two, w_up, enlarged, columns,
    plane_send, plane_recv, ring_send, ring_recv, part_send, part_recv, near_send, near_recv, weight_sem,
):
    s, g = lax.axis_index("seq"), lax.axis_index("head")
    z, row = s // ROWS, s % ROWS
    place = row * GROUPS + g
    up, down = ((s + ROWS) % SEQ, g), ((s + SEQ - ROWS) % SEQ, g)
    after, before = (s + 1) % SEQ, (s + SEQ - 1) % SEQ
    next_g, last_g = (g + 1) % GROUPS, (g + GROUPS - 1) % GROUPS

    def peer(i):
        other = (place + i) % PLACES
        return other, (z * ROWS + other // GROUPS, other % GROUPS)

    def columns_of(group):
        return pl.ds(pl.multiple_of(group * WIDE, WIDE), WIDE)

    def tokens_of(index):
        return pl.ds(pl.multiple_of(index * OWN, OWN), OWN)

    barrier = pltpu.get_barrier_semaphore()

    def greet(i, carry):
        pl.semaphore_signal(barrier, inc=1, device_id=peer(i)[1], device_id_type=MESH)
        return carry

    lax.fori_loop(1, PLACES, greet, 0)
    for other in (up, down, (after, g), (before, g), (after, last_g), (before, last_g)):
        pl.semaphore_signal(barrier, inc=1, device_id=other, device_id_type=MESH)

    weights_in = pltpu.make_async_copy(w_in_any, w_in, weight_sem.at[0])
    weights_up = pltpu.make_async_copy(w_up_any, w_up, weight_sem.at[1])
    weights_in.start()
    weights_up.start()
    for kind, source in ((0, k_in), (1, v_in)):
        pltpu.make_async_copy(
            source.at[:, columns_of(g)], kv.at[kind, 0, tokens_of(g)], plane_recv.at[kind]
        ).start()
    pltpu.make_async_copy(q_in.at[:, columns_of(g)], queries.at[tokens_of(place)], plane_recv.at[2]).start()
    pl.semaphore_wait(barrier, PLACES - 1 + 6)

    for kind, source in ((0, k_in), (1, v_in)):

        def send_row(i, carry):
            other = (g + i) % GROUPS
            pltpu.make_async_remote_copy(
                src_ref=source.at[:, columns_of(other)],
                dst_ref=kv.at[kind, 0, tokens_of(g)],
                send_sem=plane_send.at[kind],
                recv_sem=plane_recv.at[kind],
                device_id=(s, other),
                device_id_type=MESH,
            ).start()
            return carry

        lax.fori_loop(1, GROUPS, send_row, 0)

    def send_query(i, carry):
        device = peer(i)[1]
        pltpu.make_async_remote_copy(
            src_ref=q_in.at[:, columns_of(device[1])],
            dst_ref=queries.at[tokens_of(place)],
            send_sem=plane_send.at[2],
            recv_sem=plane_recv.at[2],
            device_id=device,
            device_id_type=MESH,
        ).start()
        return carry

    lax.fori_loop(1, PLACES, send_query, 0)

    def hop(kind, source, target, way):
        return pltpu.make_async_remote_copy(
            src_ref=kv.at[kind, source],
            dst_ref=kv.at[kind, target],
            send_sem=ring_send.at[way],
            recv_sem=ring_recv.at[kind, target],
            device_id=(up, down)[way],
            device_id_type=MESH,
        )

    def arrived(kind, slot):
        pltpu.make_async_copy(kv.at[kind, slot], kv.at[kind, slot], ring_recv.at[kind, slot]).wait()

    for kind in (0, 1):
        pltpu.make_async_copy(kv.at[kind, 0], kv.at[kind, 0], plane_recv.at[kind]).wait()
        hop(kind, 0, 1, 0).start()
        hop(kind, 0, 9, 1).start()

    weights_in.wait()
    w_two[...] = jnp.zeros_like(w_two)
    for t in range(3):
        for u in range(3):
            piece = w_in[(t * 3 + u) * 48 : (t * 3 + u) * 48 + 48, :]
            for half in range(2):
                at = t * 256 + (u + half) * 64
                w_two[at : at + 48, half * CH : half * CH + CH] = piece
    enlarged[...] = jnp.zeros_like(enlarged)
    turned[...] = jnp.zeros_like(turned)
    pltpu.make_async_copy(queries, queries, plane_recv.at[2]).wait()

    def attend(slots, first=False):
        for h in range(LOCAL):
            lanes = slice(h * HD, h * HD + HD)
            keys = [kv[0, slot, :, lanes] for slot in slots]
            values = [kv[1, slot, :, lanes] for slot in slots]
            keys = keys[0] if len(keys) == 1 else jnp.concatenate(keys, axis=0)
            values = values[0] if len(values) == 1 else jnp.concatenate(values, axis=0)
            for c in range(2):
                some = slice(c * 256, c * 256 + 256)
                scores = dot(keys, queries[some, lanes], ((1,), (1,)))
                new = jnp.max(scores, axis=0, keepdims=True)
                if not first:
                    old = top[h : h + 1, some]
                    new = jnp.maximum(old, new)
                    fading = jnp.exp2((old - new) * TO_LOG2)
                weights = jnp.exp2((scores - new) * TO_LOG2)
                sums = jnp.sum(weights, axis=0, keepdims=True)
                product = dot(values, weights.astype(BF16), ((0,), (0,)))
                if first:
                    total[h : h + 1, some] = sums
                    summed[lanes, some] = product
                else:
                    total[h : h + 1, some] = total[h : h + 1, some] * fading + sums
                    summed[lanes, some] = summed[lanes, some] * fading + product
                top[h : h + 1, some] = new

    attend([0], first=True)

    def step(t, carry):
        for kind in (0, 1):
            arrived(kind, t)
            hop(kind, t, t + 1, 0).start()
            arrived(kind, t + 8)
            hop(kind, t + 8, t + 9, 1).start()
        attend([t, t + 8])
        return carry

    lax.fori_loop(1, 7, step, 0)
    arrived(0, 7)
    hop(0, 7, 8, 0).start()
    arrived(0, 15)
    arrived(1, 15)
    hop(1, 15, 8, 1).start()
    arrived(1, 7)
    attend([7, 15])
    arrived(0, 8)
    arrived(1, 8)
    attend([8])

    for h in range(LOCAL):
        lanes = slice(h * HD, h * HD + HD)
        sums = total[h : h + 1, :]
        attended = (summed[lanes, :] / sums).astype(BF16)
        turned[h * PATCH : h * PATCH + PATCH, :] = dot(proj_ref[lanes, :], attended, ((0,), (0,)))
        level = top[h : h + 1, :] * TO_LOG2 + jnp.log(sums) * math.log2(math.e)
        for term in range(3):
            rounded = level.astype(BF16).astype(F32)
            turned[NUM + term * LOCAL + h : NUM + term * LOCAL + h + 1, :] = rounded
            level = level - rounded
    sending[...] = turned[...].T.astype(BF16)

    own_part = pltpu.make_async_copy(sending.at[tokens_of(place)], parts.at[tokens_of(place)], part_recv)
    own_part.start()

    def send_part(i, carry):
        other, device = peer(i)
        pltpu.make_async_remote_copy(
            src_ref=sending.at[tokens_of(other)],
            dst_ref=parts.at[tokens_of(place)],
            send_sem=part_send,
            recv_sem=part_recv,
            device_id=device,
            device_id_type=MESH,
        ).start()
        return carry

    lax.fori_loop(1, PLACES, send_part, 0)

    def ones_where(shape, made):
        r = lax.broadcasted_iota(jnp.int32, shape, 0)
        c = lax.broadcasted_iota(jnp.int32, shape, 1)
        return made(r, c).astype(F32).astype(BF16)

    spread = ones_where(
        (MSG, NUM),
        lambda r, c: (r >= NUM) & (r < NUM + 3 * LOCAL) & ((r - NUM) % LOCAL == c // PATCH),
    )
    pltpu.make_async_copy(parts, parts, part_recv).wait()

    levels = dot(parts[...], spread, ((1,), (0,)))
    values = parts[:, :NUM].astype(F32)
    by_row = [slice(r * ROW, r * ROW + ROW) for r in range(ROWS)]
    highest = levels[by_row[0]]
    for r in range(1, ROWS):
        highest = jnp.maximum(highest, levels[by_row[r]])
    above, below = 0.0, 0.0
    for r in range(ROWS):
        share = jnp.exp2(levels[by_row[r]] - highest)
        above = above + share * values[by_row[r]]
        below = below + share
    merged = above / below
    tokens = merged[:OWN]
    for other in range(1, GROUPS):
        tokens = tokens + merged[other * OWN : other * OWN + OWN]
    patch = base_ref[...].astype(F32)
    for h in range(LOCAL):
        patch = patch + tokens[:, h * PATCH : h * PATCH + PATCH]
    std = jnp.concatenate([std_ref[...]] * 4, axis=1)
    mean = jnp.concatenate([mean_ref[...]] * 4, axis=1)
    latent = patch * std + mean
    lat_own[...] = jnp.concatenate([latent, latent], axis=1).astype(BF16)

    for slot, device in enumerate(((after, next_g), (after, g), (s, next_g), (before, next_g), (before, g))):
        pltpu.make_async_remote_copy(
            src_ref=lat_own,
            dst_ref=lat_near.at[slot],
            send_sem=near_send,
            recv_sem=near_recv,
            device_id=device,
            device_id_type=MESH,
        ).start()

    def picks(b):
        def made(r, c):
            a, v, low = c // 64, (c // 16) % 4, c % 16
            spot = v + 1 - b
            wanted = (spot // 2) * 64 + a * 32 + (spot % 2) * 16 + low
            return (v < 3) & (r == wanted)

        return ones_where((128, 128), made)

    pick = [picks(0), picks(1)]
    pltpu.make_async_copy(lat_near, lat_near, near_recv).wait()

    has_before = (s > 0).astype(F32)
    has_after = (s < SEQ - 1).astype(F32)
    has_frames = (g > 0).astype(F32)
    tiles = [
        [lat_near[0].astype(F32) * (has_before * has_frames), lat_near[1].astype(F32) * has_before],
        [lat_near[2].astype(F32) * has_frames, lat_own[...].astype(F32)],
        [lat_near[3].astype(F32) * (has_after * has_frames), lat_near[4].astype(F32) * has_after],
    ]
    lane = lax.broadcasted_iota(jnp.int32, (8, 128), 1)
    line = lax.broadcasted_iota(jnp.int32, (8, 128), 0)
    sides = ([], [])
    for f in range(4):
        for r in range(3):
            here = tiles[r][f // 2][(f % 2) * 8 : (f % 2) * 8 + 8]
            left = jnp.where(line == 0, 0.0, pltpu.roll(here, 1, 0))
            right = jnp.where(line == 7, 0.0, pltpu.roll(here, 7, 0))
            sides[0].append(jnp.where(lane < 64, left, here))
            sides[1].append(jnp.where(lane < 64, here, right))
    windows = [
        dot(jnp.concatenate(side, axis=0).astype(BF16), chosen, ((1,), (0,))) for side, chosen in zip(sides, pick)
    ]

    def window(f, r, b):
        at = (f * 3 + r) * 8
        return windows[b][at : at + 8]

    lines = []
    for f in range(2):
        for pair in range(2):
            for b in range(2):
                pieces = [window(f + t, pair + r, b) for t in range(3) for r in range(2)]
                lines.append(jnp.concatenate(pieces, axis=1))
    conv = dot(jnp.concatenate(lines, axis=0).astype(BF16), w_two[...], ((1,), (0,)))
    for half in range(2):
        out = conv[:, half * CH : half * CH + CH] + b_in_ref[...]
        mean_sq = jnp.mean(out * out, axis=1, keepdims=True)
        normed = out * lax.rsqrt(mean_sq + 1e-6) * gain_ref[...]
        active = normed / (1.0 + jnp.exp(-normed))
        for f in range(2):
            for pair in range(2):
                y = 2 * pair + half
                for b in range(2):
                    at = ((f * 2 + pair) * 2 + b) * 8
                    part = active[at : at + 8]
                    if y == 0:
                        part = part * has_before
                    if y == 3:
                        part = part * has_after
                    for twice in range(2):
                        for tile in range(3):
                            enlarged[tile, f * 4 + y, pl.ds(EDGE + 2 * b + twice, 8, stride=4), :] = part[
                                :, tile * 128 : tile * 128 + 128
                            ]

    for v in range(3):
        for f in range(2):
            for y in range(4):
                piece = [enlarged[tile, f * 4 + y, EDGE - 1 + v : EDGE + 31 + v, :] for tile in range(3)]
                piece = jnp.concatenate(piece, axis=1).astype(BF16)
                for line_out in range(4):
                    for u in range(3):
                        if (line_out + u + 1) // 2 == y:
                            at = (f * 4 + line_out) * 32
                            to = (u * 3 + v) * CH
                            columns[at : at + 32, to : to + CH] = piece
    weights_up.wait()
    planes = dot(columns[...], w_up[...], ((1,), (0,))) + b_up_ref[...]
    out_ref[...] = planes.astype(BF16)

    for kind in (0, 1):
        sent = kv.at[kind, 0, : ROW - OWN]
        pltpu.make_async_copy(sent, sent, plane_send.at[kind]).wait()
    sent = queries.at[: PLANE - OWN]
    pltpu.make_async_copy(sent, sent, plane_send.at[2]).wait()
    for way in (0, 1):
        sent = kv.at[0, :15]
        pltpu.make_async_copy(sent, sent, ring_send.at[way]).wait()
    sent = parts.at[: PLANE - OWN]
    pltpu.make_async_copy(sent, sent, part_send).wait()
    pltpu.make_async_copy(lat_near, lat_near, near_send).wait()


def on_device(
    query_states,
    key_states,
    value_states,
    base_patch,
    head_proj,
    latent_std,
    latent_mean,
    w_in,
    b_in,
    gain_mid,
    w_up,
    b_up,
):
    here = pl.BlockSpec(memory_space=pltpu.VMEM)
    far = pl.BlockSpec(memory_space=pl.ANY)
    DMA = pltpu.SemaphoreType.DMA
    planes = pl.pallas_call(
        kernel,
        out_shape=jax.ShapeDtypeStruct((256, OUTCH), BF16),
        in_specs=[far, far, far, here, here, here, here, far, here, here, far, here],
        out_specs=here,
        scratch_shapes=[
            pltpu.VMEM((2, 16, ROW, WIDE), BF16),
            pltpu.VMEM((PLANE, WIDE), BF16),
            pltpu.VMEM((8, PLANE), F32),
            pltpu.VMEM((8, PLANE), F32),
            pltpu.VMEM((WIDE, PLANE), F32),
            pltpu.VMEM((MSG, PLANE), F32),
            pltpu.VMEM((PLANE, MSG), BF16),
            pltpu.VMEM((PLANE, MSG), BF16),
            pltpu.VMEM((OWN, 128), BF16),
            pltpu.VMEM((5, OWN, 128), BF16),
            pltpu.VMEM((27 * 16, CH), BF16),
            pltpu.VMEM((768, 2 * CH), BF16),
            pltpu.VMEM((9 * CH, OUTCH), BF16),
            pltpu.VMEM((3, 8, LINE, 128), F32),
            pltpu.VMEM((256, 9 * CH), BF16),
            DMA((3,)),
            DMA((3,)),
            DMA((2,)),
            DMA((2, 16)),
            DMA,
            DMA,
            DMA,
            DMA,
            DMA((2,)),
        ],
        compiler_params=pltpu.CompilerParams(
            collective_id=0, has_side_effects=True, vmem_limit_bytes=48 * 1024 * 1024
        ),
        name="attend_and_decode",
    )(
        query_states,
        key_states,
        value_states,
        base_patch,
        head_proj,
        latent_std.reshape(1, 16),
        latent_mean.reshape(1, 16),
        w_in.reshape(27 * 16, CH),
        b_in.reshape(1, CH),
        gain_mid.reshape(1, CH),
        w_up.reshape(9 * CH, OUTCH),
        b_up.reshape(1, OUTCH),
    )
    return planes.reshape(2, 4, 32, OUTCH)


def solution(mesh):
    in_specs = (
        P(("seq", "head"), None),
        P(("seq", "head"), None),
        P(("seq", "head"), None),
        P(("seq", "head"), None),
        P("head", None),
        P(),
        P(),
        P(),
        P(),
        P(),
        P(),
        P(),
    )
    out_specs = P("head", "seq", None, None)
    return jax.shard_map(
        on_device, mesh=mesh, in_specs=in_specs, out_specs=out_specs, check_vma=False
    )
```

time: 411 us -> 77.3 us (0.19); the launches traced: 404 us -> 77 us
  waiting for transfers between devices: 224 us -> 0 us
  Pallas kernels: 0 us -> 71.4 us
  blocking collectives: 53.9 us -> 0 us
  local copies, waits for them, and re-layouts: 54.8 us -> 5.55 us
  starting transfers between devices: 27.6 us -> 0 us
  matrix products: 26.8 us -> 0 us
  between operations: 13.9 us -> 0.13 us
    all_gather x2 -> x0, waiting for transfers between devices: 208 us -> none  [the longest x1 107 us: on_device(): key_piece = lax.all_gather(k_rows, 'seq', axis=0, tiled=True)]
    pallas_call x0 -> x1, Pallas kernels: none -> 71.4 us  [on_device(): pl.pallas_call(kernel, out_shape=jax.ShapeDtypeStruct((256, OUTCH), BF16)...]
    reshape x5 -> x2, local copies, waits for them, and re-layouts: 33.5 us -> 1.42 us  [the longest x1 0.74 us: on_device(): b_in.reshape(1, CH)]
    all_gather x1 -> x0, blocking collectives: 29.9 us -> none  [on_device(): full_proj = lax.all_gather(head_proj, 'head', axis=0, tiled=True)]
    dot_general x17 -> x0, matrix products: 25.4 us -> none  [the longest x8 13.1 us: one_step(): jnp.einsum('hqk,khd->hqd', weights.astype(jnp.bfloat16), value_block, pre...]
    all_to_all x2 -> x0, blocking collectives: 24 us -> none  [the longest x1 14.2 us: on_device(): lax.all_to_all(key_states, 'head', split_axis=1, concat_axis=0, tiled=True)]
    ppermute x5 -> x0, starting transfers between devices: 18.1 us -> none  [the longest x2 11.9 us: with_halo(): before = lax.ppermute(last, axis, up)]
    unnamed x26 -> x19, local copies, waits for them, and re-layouts: 15.5 us -> 4.13 us
  transfers between devices with their start and end apart: 9 -> 0, of which waited for: 6 -> 0; matrix products, arithmetic and copies ran while one was open for 7% -> 0% of each run, Pallas kernels for 0% -> 0%
where the time goes in v1:
time: 77.3 us; the launch traced here: 77 us
  Pallas kernels  71.4 us (92%)
  local copies, waits for them, and re-layouts  5.55 us (7%)
    pallas_call x1, Pallas kernels, on_device(): pl.pallas_call(kernel, out_shape=jax.ShapeDtypeStruct((256, OUTCH), BF16)...  71.4 us
    unnamed x19, local copies, waits for them, and re-layouts  4.13 us

profile of v1, /device:TPU:1, one launch (start us, length us, event | category | flops | bytes accessed | tf_op | source)
XLA Modules:
  0.0 77.0 jit_solution(18236191143185790469)
XLA Ops:
  0.0 0.0 copy-start.5
  0.0 0.0 copy-start
  0.0 0.0 copy-start.7
  0.0 0.0 copy-start.6
  0.0 0.0 copy-start.4
  0.0 0.0 copy-start.3
  0.0 0.0 copy-start.2
  0.0 0.0 copy-start.1
  0.1 0.7 reshape.27.b_in_ref
  0.8 0.7 reshape.28.gain_ref
  1.5 0.9 %copy.14.proj_ref = bf16[384,64]{1,0:T(8,128)(2,1)S(1)} copy(bf16[384,64]{0,1:T(8,128)(2,1)} %param.16) | data formatting | bytes 98304 | tf_op args[4]
  2.4 2.5 %copy.13 = bf16[3,3,384,192]{3,2,1,0:T(8,128)(2,1)S(1)} copy(bf16[3,3,384,192]{2,3,1,0:T(8,128)(2,1)} %param.22) | data formatting | bytes 2654208 | tf_op args[10]
  4.9 0.0 copy-done.5
  4.9 0.0 copy-done
  5.0 0.0 copy-done.7
  5.0 0.0 copy-done.6
  5.0 0.0 copy-done.4
  5.0 0.0 copy-done.3
  5.0 0.0 copy-done.2
  5.0 0.0 copy-done.1
  5.0 71.4 %attend_and_decode.1 = bf16[256,192]{1,0:T(8,128)(2,1)S(1)} custom-call(bf16[16,3072]{1,0:T(8,128)(2,1)S(1)} %copy-done.1, bf16[16,3072]{1,0:T(8,128)(2,1)S(1)} %copy-done.2, bf16[16,3072]{1,0:T(8,128)(2,1)S(1)} %copy-done.3, bf16[16,64]{1,0:T(8,128)(2,1)S(1)} %copy-done.4, bf16[384,64]{1,0:T(8,128)(2,1)S(1)} %copy.14.proj_ref, f32[1,16]{1,0:T(1,128)S(1)} %bitcast.10, ...), custom_call_target="tpu_custom_call" | custom-call | tf_op jit(solution)/shard_map/attend_and_decode/pallas_call | solution.py:371
  76.4 0.7 copy.16
Async XLA Ops:
  0.0 4.9 %copy-start.5 = (f32[192]{0:T(256)S(1)}, f32[192]{0:T(256)}, u32[]{:S(2)}) copy-start(f32[192]{0:T(256)} %param.23) | copy-start | bytes 2308
  0.0 4.9 %copy-start = (bf16[3,3,3,16,384]{4,3,2,1,0:T(8,128)(2,1)S(1)}, bf16[3,3,3,16,384]{4,3,2,1,0:T(8,128)(2,1)}, u32[]{:S(2)}) copy-start(bf16[3,3,3,16,384]{4,3,2,1,0:T(8,128)(2,1)} %param.19) | copy-start | bytes 995332
  0.0 5.0 %copy-start.7 = (f32[16]{0:T(128)S(1)}, f32[16]{0:T(128)}, u32[]{:S(2)}) copy-start(f32[16]{0:T(128)} %param.18) | copy-start | bytes 196
  0.0 5.0 %copy-start.6 = (f32[16]{0:T(128)S(1)}, f32[16]{0:T(128)}, u32[]{:S(2)}) copy-start(f32[16]{0:T(128)} %param.17) | copy-start | bytes 196
  0.0 5.0 %copy-start.4 = (bf16[16,64]{1,0:T(8,128)(2,1)S(1)}, bf16[16,64]{1,0:T(8,128)(2,1)}, u32[]{:S(2)}) copy-start(bf16[16,64]{1,0:T(8,128)(2,1)} %base_ref.1) | copy-start | bytes 6148
  0.0 5.0 %copy-start.3 = (bf16[16,3072]{1,0:T(8,128)(2,1)S(1)}, bf16[16,3072]{1,0:T(8,128)(2,1)}, u32[]{:S(2)}) copy-start(bf16[16,3072]{1,0:T(8,128)(2,1)} %v_in.1) | copy-start | bytes 294916
  0.0 5.0 %copy-start.2 = (bf16[16,3072]{1,0:T(8,128)(2,1)S(1)}, bf16[16,3072]{1,0:T(8,128)(2,1)}, u32[]{:S(2)}) copy-start(bf16[16,3072]{1,0:T(8,128)(2,1)} %k_in.1) | copy-start | bytes 294916
  0.0 5.0 %copy-start.1 = (bf16[16,3072]{1,0:T(8,128)(2,1)S(1)}, bf16[16,3072]{1,0:T(8,128)(2,1)}, u32[]{:S(2)}) copy-start(bf16[16,3072]{1,0:T(8,128)(2,1)} %q_in.1) | copy-start | bytes 294916
